TPU v7x, 32 devices: a whole 2x2x4 slice. The times are simulated.
32 devices in a mesh: seq: 8 (over y, x, core), tp: 4 (over z).
Axes of the slice: x: 2, y: 2, z: 4, core: 2. Of those that a mesh axis runs over, the one named last changes fastest.
Arguments:
- frames: bfloat16 [640, 8, 1024], P('tp', 'seq'), may hold values from -6 to 6
- conv_weight: bfloat16 [9, 640, 640], P(None, 'tp'), may hold values from -0.078125 to 0.078125
- time_weight: bfloat16 [3, 640, 640], P(None, 'tp'), may hold values from -0.125 to 0.125
- cotangent: bfloat16 [640, 8, 1024], P('tp', 'seq'), may hold values from -6 to 6
Outputs:
- output: bfloat16 [640, 8, 1024], P('tp', 'seq')
- frame_grad: bfloat16 [640, 8, 1024], P('tp', 'seq')
- conv_grad: float32 [9, 640, 640], P(None, 'tp')
- time_grad: float32 [3, 640, 640], P(None, 'tp')
All inputs are finite; a program needn't handle non-finite values.
Results may differ from a plain program's by a relative error of at most 0.0034.
Values may be sent and summed in bfloat16 or wider, within the bound.
A program may use at most 128 MiB of HBM per device.

v0:
```python
import jax
import jax.numpy as jnp
from jax import lax
from jax.sharding import PartitionSpec as P

HGT = 32
WID = 32


def padded_2(cells, sides, width):
    for axis, dim in sides:
        count = lax.axis_size(axis)
        ends = count - 1
        head = lax.slice_in_dim(cells, 0, width, axis=dim)
        tail = lax.slice_in_dim(cells, cells.shape[dim] - width, cells.shape[dim], axis=dim)
        cells = jnp.concatenate(
            [
                lax.ppermute(tail, axis, [(i, (i + 1) % count) for i in range(ends)]),
                cells,
                lax.ppermute(head, axis, [((i + 1) % count, i) for i in range(ends)]),
            ],
            axis=dim,
        )
    return cells


def shift_plane(field, down, right):
    leading = field.shape[:-1]
    plane = field.reshape(leading + (HGT, WID))
    padding = [(0, 0)] * len(leading) + [(1, 1), (1, 1)]
    padded = jnp.pad(plane, padding)
    moved = padded[..., 1 + down : 1 + down + HGT, 1 + right : 1 + right + WID]
    return moved.reshape(leading + (HGT * WID,))


def flatten(field):
    return field.reshape(field.shape[0], -1)


def contract_first(weight, data):
    return lax.dot_general(
        weight, data, (((0,), (0,)), ((), ())), preferred_element_type=jnp.float32
    )


def contract_last(left_side, right_side):
    return lax.dot_general(
        left_side, right_side, (((1,), (1,)), ((), ())), preferred_element_type=jnp.float32
    )


def temporal_fold(time_weight, cot_flat, frame_count):

    def add_window(carry, piece, start):
        mixed, time_part = carry
        parts = []
        for tap in range(3):
            window = flatten(piece[:, tap : tap + frame_count, :])
            weight_cols = time_weight[tap]
            mixed = mixed + jnp.dot(weight_cols, window, preferred_element_type=jnp.float32)
            parts.append(contract_last(cot_flat, window))
        time_part = jnp.stack(parts)
        return (mixed, time_part)

    return add_window


def per_device(frames, conv_weight, time_weight, cotangent):
    local_out, frame_count, plane_size = frames.shape
    total_channels = conv_weight.shape[2]
    all_frames = frame_count * lax.axis_size("seq")
    plane_zero = jnp.zeros((local_out, frame_count * plane_size), jnp.float32)
    total = plane_zero
    piece = lax.all_gather(frames, "tp", axis=0, tiled=True)
    for tap in range(9):
        moved = flatten(shift_plane(piece, tap // 3 - 1, tap % 3 - 1))
        weight_cols = conv_weight[tap]
        total = total + jnp.dot(weight_cols, moved, preferred_element_type=jnp.float32)
    pre = total.reshape(frames.shape)
    act = jax.nn.silu(pre).astype(jnp.bfloat16)
    cot_flat = flatten(cotangent)
    time_zero = jnp.zeros((3, local_out, total_channels), jnp.float32)
    rimmed = padded_2(act, (("seq", 1),), 1)
    folding = temporal_fold(time_weight, cot_flat, frame_count)
    mixed, time_part = folding(
        (plane_zero, time_zero), lax.all_gather(rimmed, "tp", axis=0, tiled=True), jnp.int32(0)
    )
    mixed = mixed.reshape(frames.shape)
    output = (frames.astype(jnp.float32) + mixed).astype(jnp.bfloat16)
    cot_rims = padded_2(cotangent, (("seq", 1),), 1)
    count_rows = lax.axis_size("tp") * local_out
    total = jnp.zeros((count_rows, frame_count * plane_size), jnp.float32)
    for tap in range(3):
        window = flatten(cot_rims[:, 2 - tap : 2 - tap + frame_count, :])
        weight_cols = time_weight[tap]
        total = total + contract_first(weight_cols, window)
    back = lax.psum_scatter(
        total.reshape(count_rows, frame_count, plane_size), "tp", scatter_dimension=0, tiled=True
    )
    sigmoid_pre = jax.nn.sigmoid(pre)
    slope = sigmoid_pre * (1.0 + pre * (1.0 - sigmoid_pre))
    pre_grad = (back * slope).astype(jnp.bfloat16)
    pre_flat = flatten(pre_grad)
    count_rows = lax.axis_size("tp") * local_out
    total = jnp.zeros((count_rows, frame_count, plane_size), jnp.float32)
    for tap in range(9):
        down = tap // 3 - 1
        right = tap % 3 - 1
        weight_cols = conv_weight[tap]
        spread = contract_first(weight_cols, pre_flat).reshape(count_rows, frame_count, plane_size)
        total = total + shift_plane(spread, -down, -right)
    frame_grad = (
        cotangent.astype(jnp.float32)
        + lax.psum_scatter(total, "tp", scatter_dimension=0, tiled=True)
    ).astype(jnp.bfloat16)
    piece = lax.all_gather(frames, "tp", axis=0, tiled=True)
    parts = []
    for tap in range(9):
        moved = flatten(shift_plane(piece, tap // 3 - 1, tap % 3 - 1))
        parts.append(contract_last(pre_flat, moved))
    conv_part = jnp.stack(parts)
    summed = lax.psum((conv_part, time_part), "seq")
    return (output, frame_grad, summed[0] / all_frames, summed[1] / all_frames)


def solution(mesh):
    placed = (P("tp", "seq", None), P(None, "tp", None), P(None, "tp", None), P("tp", "seq", None))
    return jax.shard_map(
        per_device,
        mesh=mesh,
        in_specs=placed,
        out_specs=(
            P("tp", "seq", None),
            P("tp", "seq", None),
            P(None, "tp", None),
            P(None, "tp", None),
        ),
        check_vma=False,
    )
```

profile of v0, /device:TPU:1, one launch (start us, length us, event | category | flops | bytes accessed | tf_op | source)
XLA Modules:
  0.0 385.6 jit_solution(4481947461480605136)
XLA Ops:
  8.0 2.0 collective-permute-start.2
  9.9 4.5 %collective-permute-start.3 = (bf16[160,1,1024]{2,0,1:T(8,128)(2,1)}, bf16[160,1,1024]{2,0,1:T(8,128)(2,1)S(1)}, u32[]{:S(2)}, u32[]{:S(2)}) collective-permute-start(bf16[160,1,1024]{2,0,1:T(8,128)(2,1)} %param.7), channel_id=1, source_target_pairs={{0,4},{4,8},{8,12},{12,16},{16,20},{20,24},{24,28},{1,5},{5,9},{9,... | collective-permute-start | bytes 983048 | tf_op jit(solution)/shard_map/ppermute | solution.py:18
  14.4 1.6 fusion.69
  16.0 1.4 collective-permute-done.2
  18.7 2.0 add_bitcast_fusion
  20.8 22.9 %all-gather.3.cloned.1.call-done = bf16[640,1,1024]{2,0,1:T(8,128)(2,1)} async-done(((bf16[160,1,1024]{2,0,1:T(8,128)(2,1)}), bf16[640,1,1024]{2,0,1:T(8,128)(2,1)}) %all-gather.3.cloned.1.call-update) | async-done | bytes 1310736 | tf_op jit(solution)/shard_map/all_gather | solution.py:74
  43.7 1.7 copy.13
  45.5 3.9 %pad_slice_fusion.11 = (bf16[640,1,32,32]{0,3,2,1:T(8,128)(2,1)S(1)}, bf16[640,1,32,32]{0,3,2,1:T(8,128)(2,1)S(1)}, bf16[640,1,32,32]{0,3,2,1:T(8,128)(2,1)S(1)}...) fusion(bf16[640,1,32,32]{0,3,2,1:T(8,128)(2,1)S(1)} %bitcast.327), kind=kLoop, calls=%fused_computation.21 | loop fusion | bytes 11796480 | tf_op jit(solution)/shard_map/slice | solution.py:32
  56.5 4.3 %collective-permute-start = (bf16[160,1,1024]{2,0,1:T(8,128)(2,1)S(1)}, bf16[160,1,1024]{2,0,1:T(8,128)(2,1)S(1)}, u32[]{:S(2)}, u32[]{:S(2)}) collective-permute-start(bf16[160,1,1024]{2,0,1:T(8,128)(2,1)S(1)} %fusion.73), channel_id=1, source_target_pairs={{0,4},{4,8},{8,12},{12,16},{16,20},{20,24},{24,28},{1,5},{5,9},{9,... | collective-permute-start | bytes 983048 | tf_op jit(solution)/shard_map/ppermute | solution.py:18
  60.7 1.9 collective-permute-start.1
  62.7 2.1 collective-permute-done
  64.7 5.5 %collective-permute-done.1 = bf16[160,1,1024]{2,0,1:T(8,128)(2,1)S(1)} collective-permute-done((bf16[160,1,1024]{2,0,1:T(8,128)(2,1)S(1)}, bf16[160,1,1024]{2,0,1:T(8,128)(2,1)S(1)}, u32[]{:S(2)}, u32[]{:S(2)}) %collective-permute-start.1) | collective-permute-done | bytes 327712 | tf_op jit(solution)/shard_map/ppermute | solution.py:20
  71.6 26.8 %reduce-scatter.2.cloned.1.call-done = f32[160,1,1024]{2,0,1:T(8,128)} async-done(((f32[640,1,1024]{2,0,1:T(8,128)}), f32[160,1,1024]{2,0,1:T(8,128)}) %reduce-scatter.2.cloned.1.call-update) | async-done | bytes 655376 | tf_op jit(solution)/shard_map/reduce_scatter | solution.py:97
  98.4 1.5 fusion.35
  99.9 1.7 fusion.60
  108.3 2.5 fusion.3
  110.8 6.5 %copy.15 = f32[640,1,1024]{2,1,0:T(1,128)} copy(f32[640,1,1024]{0,2,1:T(8,128)} %fusion.3) | data formatting | bytes 5242880 | tf_op jit(solution)/shard_map/add | solution.py:111
  117.3 2.6 fusion.32
  119.9 1.2 fusion.31
  121.4 2.6 fusion.30
  124.1 1.2 fusion.29
  125.2 1.3 fusion.22
  128.9 1.2 fusion.26
  131.3 45.4 %all-gather.5.cloned.1.call-done = bf16[640,3,1024]{2,0,1:T(8,128)(2,1)} async-done(((bf16[160,3,1024]{2,0,1:T(8,128)(2,1)}), bf16[640,3,1024]{2,0,1:T(8,128)(2,1)}) %all-gather.5.cloned.1.call-update) | async-done | bytes 3932176 | tf_op jit(solution)/shard_map/all_gather | solution.py:86
  176.7 1.9 convolution_bitcast_fusion.4
  178.6 1.9 convolution_bitcast_fusion.5
  180.5 1.9 convolution_bitcast_fusion.6
  185.4 96.2 %all-reduce.14.cloned.1.call-done = f32[640,1,1024]{2,1,0:T(1,128)} async-done(((f32[640,1,1024]{2,1,0:T(1,128)}), f32[640,1,1024]{2,1,0:T(1,128)}) %all-reduce.14.cloned.1.call-update) | async-done | bytes 2621456
  281.6 1.9 fusion.34
  284.4 1.7 fusion.33
  288.3 85.5 %all-reduce.16.cloned.1.call-done = (f32[9,160,640]{2,1,0:T(8,128)}, f32[3,160,640]{2,1,0:T(8,128)}) async-done(((f32[9,160,640]{2,1,0:T(8,128)}, f32[3,160,640]{2,1,0:T(8,128)}), (f32[9,160,640]{2,1,0:T(8,128)}, f32[3,160,640]{2,1,0:T(8,128)})) %all-reduce.16.cloned.1.call-update) | async-done | bytes 4915216 | tf_op jit(solution)/shard_map/psum | solution.py:122
  373.8 4.2 %broadcast_multiply_fusion = f32[9,160,640]{2,1,0:T(8,128)} fusion(f32[9,160,640]{2,1,0:T(8,128)} %get-tuple-element.16), kind=kLoop, calls=%fused_computation.17 | loop fusion | flops 921600 | bytes 7372800 | tf_op jit(solution)/shard_map/div | solution.py:123
  (88 shorter events, 27.2 us)
Async XLA Ops:
  7.2 10.3 %copy-start.17 = (bf16[3,160,640]{2,1,0:T(8,128)(2,1)S(1)}, bf16[3,160,640]{2,1,0:T(8,128)(2,1)}, u32[]{:S(2)}) copy-start(bf16[3,160,640]{2,1,0:T(8,128)(2,1)} %param.6) | copy-start | bytes 1843204
  7.2 36.6 %all-gather.3.cloned.1.call-start = ((), (), s32[]{:S(2)}) async-start(), calls=%async_computation.1 | async-start | bytes 1638400 | tf_op jit(solution)/shard_map/all_gather | solution.py:74
  7.9 90.5 %reduce-scatter.2.cloned.1.call-start = ((), (), s32[]{:S(2)}) async-start(), calls=%async_computation.3 | async-start | bytes 3276800 | tf_op jit(solution)/shard_map/reduce_scatter | solution.py:97
  8.0 9.5 %collective-permute-start.2 = (bf16[160,1,1024]{2,0,1:T(8,128)(2,1)}, bf16[160,1,1024]{2,0,1:T(8,128)(2,1)S(1)}, u32[]{:S(2)}, u32[]{:S(2)}) collective-permute-start(bf16[160,1,1024]{2,0,1:T(8,128)(2,1)} %param.7), channel_id=1, source_target_pairs={{4,0},{8,4},{12,8},{16,12},{20,16},{24,20},{28,24},{5,1},{9,5},{13... | collective-permute-start | bytes 983048 | tf_op jit(solution)/shard_map/ppermute | solution.py:20
  9.9 8.8 %collective-permute-start.3 = (bf16[160,1,1024]{2,0,1:T(8,128)(2,1)}, bf16[160,1,1024]{2,0,1:T(8,128)(2,1)S(1)}, u32[]{:S(2)}, u32[]{:S(2)}) collective-permute-start(bf16[160,1,1024]{2,0,1:T(8,128)(2,1)} %param.7), channel_id=1, source_target_pairs={{0,4},{4,8},{8,12},{12,16},{16,20},{20,24},{24,28},{1,5},{5,9},{9,... | collective-permute-start | bytes 983048 | tf_op jit(solution)/shard_map/ppermute | solution.py:18
  20.8 155.9 %all-gather.5.cloned.1.call-start = ((), (), s32[]{:S(2)}) async-start(), calls=%async_computation.2 | async-start | bytes 4915200 | tf_op jit(solution)/shard_map/all_gather | solution.py:86
  45.4 4.0 %copy-start.13 = (bf16[9,160,640]{2,1,0:T(8,128)(2,1)S(1)}, bf16[9,160,640]{2,1,0:T(8,128)(2,1)}, u32[]{:S(2)}) copy-start(bf16[9,160,640]{2,1,0:T(8,128)(2,1)} %param.5) | copy-start | bytes 5529604
  49.4 1.2 copy-start.1
  49.4 1.8 copy-start.3
  49.4 2.4 copy-start.10
  49.4 3.0 copy-start.12
  49.4 3.0 copy-start.9
  49.4 3.6 copy-start.7
  49.4 5.4 %copy-start.5 = (bf16[640,1,32,32]{0,3,2,1:T(8,128)(2,1)}, bf16[640,1,32,32]{0,3,2,1:T(8,128)(2,1)S(1)}, u32[]{:S(2)}) copy-start(bf16[640,1,32,32]{0,3,2,1:T(8,128)(2,1)S(1)} %get-tuple-element.18) | copy-start | bytes 3932164
  53.0 1.3 copy-start
  55.4 0.8 copy-start.15
  56.5 8.3 %collective-permute-start = (bf16[160,1,1024]{2,0,1:T(8,128)(2,1)S(1)}, bf16[160,1,1024]{2,0,1:T(8,128)(2,1)S(1)}, u32[]{:S(2)}, u32[]{:S(2)}) collective-permute-start(bf16[160,1,1024]{2,0,1:T(8,128)(2,1)S(1)} %fusion.73), channel_id=1, source_target_pairs={{0,4},{4,8},{8,12},{12,16},{16,20},{20,24},{24,28},{1,5},{5,9},{9,... | collective-permute-start | bytes 983048 | tf_op jit(solution)/shard_map/ppermute | solution.py:18
  60.7 9.5 %collective-permute-start.1 = (bf16[160,1,1024]{2,0,1:T(8,128)(2,1)S(1)}, bf16[160,1,1024]{2,0,1:T(8,128)(2,1)S(1)}, u32[]{:S(2)}, u32[]{:S(2)}) collective-permute-start(bf16[160,1,1024]{2,0,1:T(8,128)(2,1)S(1)} %fusion.73), channel_id=1, source_target_pairs={{4,0},{8,4},{12,8},{16,12},{20,16},{24,20},{28,24},{5,1},{9,5},{13... | collective-permute-start | bytes 983048 | tf_op jit(solution)/shard_map/ppermute | solution.py:20
  71.4 210.3 %all-reduce.14.cloned.1.call-start = ((), (), s32[]{:S(2)}) async-start(), calls=%async_computation.4 | async-start | bytes 5242880
  99.9 1.7 copy-start.14
  117.3 2.6 copy-start.11
  121.2 252.6 %all-reduce.16.cloned.1.call-start = ((), (), s32[]{:S(2)}) async-start(), calls=%async_computation.5 | async-start | bytes 9830400 | tf_op jit(solution)/shard_map/psum | solution.py:122
  121.4 2.6 copy-start.8
  124.0 2.5 copy-start.6
  125.2 2.5 copy-start.4
  126.6 2.4 copy-start.2
  128.9 47.8 %copy-start.19 = (bf16[160,1,1024]{2,0,1:T(8,128)(2,1)S(1)}, bf16[160,1,1024]{2,0,1:T(8,128)(2,1)}, u32[]{:S(2)}) copy-start(bf16[160,1,1024]{2,0,1:T(8,128)(2,1)} %param.7) | copy-start | bytes 983044
  183.5 0.7 copy-start.22
  183.5 100.8 %copy-start.18 = (bf16[3,160,640]{2,1,0:T(8,128)(2,1)S(1)}, bf16[3,160,640]{2,1,0:T(8,128)(2,1)}, u32[]{:S(2)}) copy-start(bf16[3,160,640]{2,1,0:T(8,128)(2,1)} %param.6) | copy-start | bytes 1843204
  281.6 4.5 %copy-start.16 = (bf16[640,3,1024]{2,0,1:T(8,128)(2,1)S(1)}, bf16[640,3,1024]{2,0,1:T(8,128)(2,1)}, u32[]{:S(2)}) copy-start(bf16[640,3,1024]{2,0,1:T(8,128)(2,1)} %all-gather.5.cloned.1.call-done) | copy-start | bytes 11796484
  286.1 1.0 copy-start.20
  373.8 4.3 %copy-start.21 = (f32[3,160,640]{2,1,0:T(8,128)S(1)}, f32[3,160,640]{2,1,0:T(8,128)}, u32[]{:S(2)}) copy-start(f32[3,160,640]{2,1,0:T(8,128)} %get-tuple-element.17) | copy-start | bytes 3686404
Sparse Core Ops, SparseCore 0:
  9.6 34.1 all-gather.2
  46.6 51.7 reduce-scatter.1
  100.5 76.1 all-gather.4
  179.0 102.6 all-reduce.13
  285.4 88.2 all-reduce.15
where the time goes:
time: 387 us; the launch traced here: 386 us
  waiting for transfers between devices  287 us (74%)
  matrix products  40.6 us (10%)
  local copies, waits for them, and re-layouts  17.6 us (5%)
  between operations  14.9 us (4%)
  starting transfers between devices  13.2 us (3%)
  other arithmetic  12.1 us (3%)
    unnamed x6, waiting for transfers between devices  97 us
    psum x1, waiting for transfers between devices, per_device(): summed = lax.psum((conv_part, time_part), 'seq')  85.5 us
    all_gather x1, waiting for transfers between devices, per_device(): lax.all_gather(rimmed, 'tp', axis=0, tiled=True)  45.4 us
    reduce_scatter x1, waiting for transfers between devices, per_device(): lax.psum_scatter(total.reshape(count_rows, frame_count, plane_size), 'tp'...  26.8 us
    all_gather x1, waiting for transfers between devices, per_device(): piece = lax.all_gather(frames, 'tp', axis=0, tiled=True)  22.9 us
    dot_general x12, matrix products, contract_last(): lax.dot_general(left_side, right_side, (((1,), (1,)), ((), ())), preferre...  19.3 us
    dot_general x12, matrix products, contract_first(): lax.dot_general(weight, data, (((0,), (0,)), ((), ())), preferred_element...  12.8 us
    ppermute x2, starting transfers between devices, padded_2(): lax.ppermute(tail, axis, [(i, (i + 1) % count) for i in range(ends)])  8.75 us
  transfers between devices with their start and end apart: 9, of which 9 were waited for; matrix products, arithmetic and copies ran while one was open for 16% of the time, Pallas kernels for 0%

commit v1 on v0

v1 whole, which is shorter than its diff:
```python
import functools

import jax
import jax.numpy as jnp
from jax import lax
from jax.experimental import pallas as pl
from jax.experimental.pallas import tpu as pltpu
from jax.sharding import PartitionSpec as P

HGT = 32
WID = 32
BF = jnp.bfloat16
F32 = jnp.float32


def moved(x, down, right):
    if down == 0 and right == 0:
        return x
    plane = x.shape[-1]
    step = (-(WID * down + right)) % plane
    out = pltpu.roll(x, step, 1)
    where = lax.broadcasted_iota(jnp.int32, (1, plane), 1)
    row = where // WID + down
    col = where % WID + right
    ok = (row >= 0) & (row < HGT) & (col >= 0) & (col < WID)
    return jnp.where(ok, out, 0.0)


def nt(a, b):
    return lax.dot_general(a, b, (((1,), (1,)), ((), ())), preferred_element_type=F32)


def tn(a, b):
    return lax.dot_general(a, b, (((0,), (0,)), ((), ())), preferred_element_type=F32)


def nn(a, b):
    return jnp.dot(a, b, preferred_element_type=F32)


def kernel(
    ns, nz, q,
    fr, cw, tw, twt, cot,
    out, fgrad, cgrad, tgrad,
    ffull, cfull, afull, twr, chalo, prod, pre, qself, qsend, qrecv, ysend, yrecv,
    shifted, g, gsib, halfb, xin, full, fgsend, fgrecv,
    s_f, r_f, s_c, r_c, s_t, r_t, s_a, r_a, s_g, r_g,
    s_h, r_h, s_q, r_q, s_y, r_y, s_core, r_core, s_x, r_x, s_ag, r_ag, s_fw, r_fw,
):
    me = lax.axis_index("seq")
    z = lax.axis_index("tp")
    core = lax.rem(me, 2)
    chip = me // 2
    nc = ns // 2
    hr = nc * q
    loc = fr.shape[0]
    chans = nz * loc

    def zpeer(d):
        return {"tp": lax.rem(z + d, nz)}

    def speer(d):
        return {"seq": lax.rem(me + d + ns, ns)}

    def cpeer(d):
        return {"seq": lax.rem(chip + d, nc) * 2 + core}

    sib = {"seq": chip * 2 + (1 - core)}

    def remote(src, dst, ssem, rsem, dev):
        return pltpu.make_async_remote_copy(
            src_ref=src, dst_ref=dst, send_sem=ssem, recv_sem=rsem,
            device_id=dev, device_id_type=pl.DeviceIdType.MESH,
        )

    barrier = pltpu.get_barrier_semaphore()
    for d in range(1, nz):
        pl.semaphore_signal(barrier, inc=1, device_id=zpeer(d), device_id_type=pl.DeviceIdType.MESH)
    for d in range(1, ns):
        pl.semaphore_signal(barrier, inc=1, device_id=speer(d), device_id_type=pl.DeviceIdType.MESH)
    pl.semaphore_wait(barrier, nz - 1 + ns - 1)

    everything = []

    def go(copies):
        for c in copies:
            c.start()
        everything.extend(copies)
        return copies

    def arrived(copies):
        for c in copies:
            c.wait_recv()

    order = [1, nz - 1] + list(range(2, nz - 1))
    cf = go([remote(fr, ffull.at[z], s_f.at[d], r_f.at[d], zpeer(d)) for d in order])
    cc = go([remote(cot, cfull.at[z], s_c.at[d], r_c.at[d], zpeer(d)) for d in order])
    ct = go([
        remote(twt.at[lax.rem(z + d, nz)], twr.at[z], s_t.at[d], r_t.at[d], zpeer(d))
        for d in order
    ])
    ch = go([
        remote(cot, chalo.at[0], s_h.at[0], r_h.at[0], speer(1)),
        remote(cot, chalo.at[1], s_h.at[1], r_h.at[1], speer(-1)),
    ])
    ffull[z] = fr[...]
    cfull[z] = cot[...]
    twr[z] = twt[z]
    if 2 * hr > 3 * loc:
        for k in range(4):
            g[k, pl.ds(3 * loc, 2 * hr - 3 * loc), :] = jnp.zeros(
                (2 * hr - 3 * loc, chans), F32
            )
    arrived(cf)

    @pl.loop(0, 9)
    def _(t):
        prod[t] = nn(cw[t], ffull[...].reshape(chans, -1))

    total = prod[4]
    for t in range(9):
        if t != 4:
            total = total + moved(prod[t], t // 3 - 1, t % 3 - 1)
    pre[...] = total
    afull[z] = (total / (1.0 + jnp.exp(-total))).astype(BF)
    ca = go([remote(afull.at[z], afull.at[z], s_a.at[d], r_a.at[d], zpeer(d)) for d in order])

    arrived(cc)
    arrived(ct)

    def back_of(k):
        acc = nn(twr[0, k], cfull[0])
        for i in range(1, nz):
            acc = acc + nn(twr[i, k], cfull[i])
        return acc

    qsend[0] = back_of(0)
    qsend[1] = back_of(2)
    cq = go([
        remote(qsend.at[0], qrecv.at[0], s_q.at[0], r_q.at[0], speer(-1)),
        remote(qsend.at[1], qrecv.at[1], s_q.at[1], r_q.at[1], speer(1)),
    ])
    qself[...] = back_of(1)
    arrived(cq)
    back = qself[...]
    back = back + jnp.where(me < ns - 1, qrecv[0], 0.0)
    back = back + jnp.where(me > 0, qrecv[1], 0.0)
    pr = pre[...]
    sg = 1.0 / (1.0 + jnp.exp(-pr))
    pg = (back * sg * (1.0 + pr * (1.0 - sg))).astype(BF).astype(F32)
    for t in range(9):
        shifted[t] = moved(pg, 1 - t // 3, 1 - t % 3).astype(BF)

    other = pl.ds(pl.multiple_of((1 - core) * hr, 16), hr)
    mine = pl.ds(pl.multiple_of(core * hr, 16), hr)

    def core_send(k):
        return go([
            remote(g.at[k, other], gsib.at[k], s_core.at[k], r_core.at[k], sib)
        ])

    def chip_send(k):
        gsib[k] = g[k, mine, :] + gsib[k]
        halfb[k] = gsib[k].astype(BF)
        return go([
            remote(
                halfb.at[k, pl.ds(pl.multiple_of(lax.rem(chip + d, nc) * q, 16), q)],
                xin.at[k, d - 1], s_x.at[k, d - 1], r_x.at[k, d - 1], cpeer(d),
            )
            for d in range(1, nc)
        ])

    def chip_sum(k):
        acc = gsib[k, pl.ds(pl.multiple_of(chip * q, 16), q), :]
        for d in range(1, nc):
            acc = acc + xin[k, d - 1].astype(F32)
        own = pl.ds(pl.multiple_of(core * hr + chip * q, 16), q)
        full[k, own, :] = acc.astype(BF)
        return go([
            remote(
                full.at[k, own], full.at[k, own],
                s_ag.at[k, d - 1], r_ag.at[k, d - 1], cpeer(d),
            )
            for d in range(1, nc)
        ])

    def forward(k):
        return go([
            remote(full.at[k, mine], full.at[k, mine], s_fw.at[k], r_fw.at[k], sib)
        ])

    ccore, cx, cag, cfw = {}, {}, {}, {}
    for u in range(3):
        @pl.loop(0, 3)
        def _(v):
            g[u, pl.ds(pl.multiple_of(v * loc, 16), loc), :] = nt(
                shifted[3 * u + v], ffull[...].reshape(chans, -1)
            )
        ccore[u] = core_send(u)
        if u > 0:
            arrived(ccore[u - 1])
            cx[u - 1] = chip_send(u - 1)

    arrived(ca)
    arrived(ch)

    def time_part(k, rows):
        g[3, pl.ds(k * loc, loc), :] = nt(rows, afull[...].reshape(chans, -1))

    time_part(0, jnp.where(me < ns - 1, chalo[1], jnp.zeros_like(chalo[1])))
    time_part(1, cot[...])
    time_part(2, jnp.where(me > 0, chalo[0], jnp.zeros_like(chalo[0])))
    ccore[3] = core_send(3)
    arrived(ccore[2])
    cx[2] = chip_send(2)

    ysend[0] = nn(tw[0], afull[...].reshape(chans, -1)).astype(BF)
    ysend[1] = nn(tw[2], afull[...].reshape(chans, -1)).astype(BF)
    cy = go([
        remote(ysend.at[0], yrecv.at[0], s_y.at[0], r_y.at[0], speer(1)),
        remote(ysend.at[1], yrecv.at[1], s_y.at[1], r_y.at[1], speer(-1)),
    ])
    arrived(ccore[3])
    cx[3] = chip_send(3)

    prod[0:nz] = tn(cw[0], shifted[0]).reshape(nz, loc, -1)

    @pl.loop(1, 9)
    def _(t):
        prod[0:nz] += tn(cw[t], shifted[t]).reshape(nz, loc, -1)

    for i in range(nz):
        fgsend[i] = prod[i].astype(BF)
    cg = go([
        remote(fgsend.at[lax.rem(z + d, nz)], fgrecv.at[d - 1], s_g.at[d], r_g.at[d], zpeer(d))
        for d in order
    ])
    for k in range(4):
        arrived(cx[k])
        cag[k] = chip_sum(k)

    mix = nn(tw[1], afull[...].reshape(chans, -1))
    arrived(cy)
    mix = mix + jnp.where(me > 0, yrecv[0].astype(F32), 0.0)
    mix = mix + jnp.where(me < ns - 1, yrecv[1].astype(F32), 0.0)
    out[...] = (fr[...].astype(F32) + mix).astype(BF)

    for k in range(4):
        arrived(cag[k])
        cfw[k] = forward(k)

    arrived(cg)
    acc = cot[...].astype(F32) + prod[z]
    for d in range(nz - 1):
        acc = acc + fgrecv[d].astype(F32)
    fgrad[...] = acc.astype(BF)

    for k in range(4):
        arrived(cfw[k])
        for v in range(3):
            piece = full[k, v * loc:(v + 1) * loc, :].astype(F32) / ns
            if k < 3:
                cgrad[3 * k + v] = piece
            else:
                tgrad[v] = piece
    for c in everything:
        c.wait_send()


def per_device(frames, conv_weight, time_weight, cotangent):
    loc, count, plane = frames.shape
    ns, nz = lax.axis_size("seq"), lax.axis_size("tp")
    chans = conv_weight.shape[2]
    q = 16 * (-(-3 * loc // (16 * ns)))
    nc = ns // 2
    hr = nc * q
    twt = jnp.transpose(time_weight.reshape(3, loc, nz, loc), (2, 0, 3, 1))
    dma = pltpu.SemaphoreType.DMA
    V = pltpu.VMEM
    sems = [dma((nz,))] * 10 + [dma((2,))] * 6 + [dma((4,))] * 2
    sems += [dma((4, nc - 1))] * 4 + [dma((4,))] * 2
    outs = pl.pallas_call(
        functools.partial(kernel, ns, nz, q),
        out_shape=(
            jax.ShapeDtypeStruct((loc, plane), BF),
            jax.ShapeDtypeStruct((loc, plane), BF),
            jax.ShapeDtypeStruct((9, loc, chans), F32),
            jax.ShapeDtypeStruct((3, loc, chans), F32),
        ),
        in_specs=[pl.BlockSpec(memory_space=pltpu.VMEM)] * 5,
        out_specs=(pl.BlockSpec(memory_space=pltpu.VMEM),) * 4,
        scratch_shapes=[
            V((nz, loc, plane), BF),
            V((nz, loc, plane), BF),
            V((nz, loc, plane), BF),
            V((nz, 3, loc, loc), BF),
            V((2, loc, plane), BF),
            V((9, loc, plane), F32),
            V((loc, plane), F32),
            V((loc, plane), F32),
            V((2, loc, plane), F32),
            V((2, loc, plane), F32),
            V((2, loc, plane), BF),
            V((2, loc, plane), BF),
            V((9, loc, plane), BF),
            V((4, 2 * hr, chans), F32),
            V((4, hr, chans), F32),
            V((4, hr, chans), BF),
            V((4, nc - 1, q, chans), BF),
            V((4, 2 * hr, chans), BF),
            V((nz, loc, plane), BF),
            V((nz - 1, loc, plane), BF),
        ] + sems,
        compiler_params=pltpu.CompilerParams(
            collective_id=0, has_side_effects=True, vmem_limit_bytes=58 * 1024 * 1024
        ),
    )(
        frames.reshape(loc, plane), conv_weight, time_weight, twt,
        cotangent.reshape(loc, plane),
    )
    return (
        outs[0].reshape(frames.shape), outs[1].reshape(frames.shape), outs[2], outs[3],
    )


def solution(mesh):
    placed = (P("tp", "seq", None), P(None, "tp", None), P(None, "tp", None), P("tp", "seq", None))
    return jax.shard_map(
        per_device,
        mesh=mesh,
        in_specs=placed,
        out_specs=(
            P("tp", "seq", None),
            P("tp", "seq", None),
            P(None, "tp", None),
            P(None, "tp", None),
        ),
        check_vma=False,
    )
```

time: 387 us -> 178 us (0.46)
  waiting for transfers between devices: 287 us -> 0 us
  Pallas kernels: 0 us -> 163 us
  matrix products: 40.6 us -> 0 us
  between operations: 14.9 us -> 0.65 us
  starting transfers between devices: 13.2 us -> 0 us
  other arithmetic: 12.1 us -> 0 us
  local copies, waits for them, and re-layouts: 17.6 us -> 13.4 us
    pallas_call x0 -> x1, Pallas kernels: none -> 163 us  [per_device(): pl.pallas_call(functools.partial(kernel, ns, nz, q), out_shape=(jax.Shape...]
    unnamed x6 -> x0, waiting for transfers between devices: 97 us -> none
    psum x1 -> x0, waiting for transfers between devices: 85.5 us -> none  [per_device(): summed = lax.psum((conv_part, time_part), 'seq')]
    all_gather x2 -> x0, waiting for transfers between devices: 68.3 us -> none  [the longest x1 45.4 us: per_device(): lax.all_gather(rimmed, 'tp', axis=0, tiled=True)]
    dot_general x36 -> x0, matrix products: 40.6 us -> none  [the longest x12 19.3 us: contract_last(): lax.dot_general(left_side, right_side, (((1,), (1,)), ((), ())), preferre...]
    reduce_scatter x1 -> x0, waiting for transfers between devices: 26.8 us -> none  [per_device(): lax.psum_scatter(total.reshape(count_rows, frame_count, plane_size), 'tp'...]
    ppermute x4 -> x0, starting transfers between devices: 12.6 us -> none  [the longest x2 8.75 us: padded_2(): lax.ppermute(tail, axis, [(i, (i + 1) % count) for i in range(ends)])]
    ppermute x4 -> x0, waiting for transfers between devices: 9.74 us -> none  [the longest x2 6.93 us: padded_2(): lax.ppermute(head, axis, [((i + 1) % count, i) for i in range(ends)])]
  transfers between devices with their start and end apart: 9 -> 0, of which waited for: 9 -> 0; matrix products, arithmetic and copies ran while one was open for 16% -> 0% of each run, Pallas kernels for 0% -> 0%
where the time goes in v1:
time: 178 us; the launch traced here: 177 us
  Pallas kernels  163 us (92%)
  local copies, waits for them, and re-layouts  13.4 us (8%)
    pallas_call x1, Pallas kernels, per_device(): pl.pallas_call(functools.partial(kernel, ns, nz, q), out_shape=(jax.Shape...  163 us
    unnamed x6, local copies, waits for them, and re-layouts  8.69 us
    reshape x2, local copies, waits for them, and re-layouts, per_device(): twt = jnp.transpose(time_weight.reshape(3, loc, nz, loc), (2, 0, 3, 1))  4.71 us

profile of v1, /device:TPU:1, one launch (start us, length us, event | category | flops | bytes accessed | tf_op | source)
XLA Modules:
  0.0 177.4 jit_solution(9055063726054379754)
XLA Ops:
  0.6 2.7 %reshape.24 = bf16[3,160,4,160]{3,2,1,0:T(4,128)(2,1)S(1)} reshape(bf16[3,160,640]{2,1,0:T(8,128)(2,1)} %tw.1) | data formatting | bytes 1228800 | tf_op jit(solution)/shard_map/reshape | solution.py:277
  3.3 2.0 %copy.8 = bf16[3,160,4,160]{1,3,0,2:T(8,128)(2,1)} copy(bf16[3,160,4,160]{3,2,1,0:T(4,128)(2,1)S(1)} %reshape.24) | data formatting | bytes 1228800 | tf_op jit(solution)/shard_map/reshape | solution.py:277
  5.3 163.4 %shard_map.75 = (bf16[160,1024]{1,0:T(8,128)(2,1)}, bf16[160,1024]{1,0:T(8,128)(2,1)}, f32[9,160,640]{2,1,0:T(8,128)}, f32[3,160,640]{2,1,0:T(8,128)}) custom-call(bf16[160,1024]{1,0:T(8,128)(2,1)} %bitcast.8, bf16[9,160,640]{2,1,0:T(8,128)(2,1)} %cw.1, bf16[3,160,640]{2,1,0:T(8,128)(2,1)} %tw.1, bf16[4,3,160,160]{3,2,1,0:T(8,128)(2,1)} %bitcast.5, ...), custom_call_target="tpu_custom_call" | custom-call | tf_op jit(solution)/shard_map/pallas_call | solution.py:282
  168.7 1.7 copy.13
  170.4 1.7 copy.14
  172.1 0.0 copy-start
  172.2 4.2 %copy.15 = f32[9,160,640]{2,1,0:T(8,128)} copy(f32[9,160,640]{2,1,0:T(8,128)} %get-tuple-element.18) | data formatting | bytes 7372800
  176.4 0.0 copy-done
  176.4 1.0 copy.16
Async XLA Ops:
  172.1 4.2 %copy-start = (f32[3,160,640]{2,1,0:T(8,128)S(1)}, f32[3,160,640]{2,1,0:T(8,128)}, u32[]{:S(2)}) copy-start(f32[3,160,640]{2,1,0:T(8,128)} %get-tuple-element.19) | copy-start | bytes 3686404

commit v2 on v1

--- a/solution.py
+++ b/solution.py
@@ -42,10 +42,10 @@
     ns, nz, q,
     fr, cw, tw, twt, cot,
     out, fgrad, cgrad, tgrad,
-    ffull, cfull, afull, twr, chalo, prod, pre, qself, qsend, qrecv, ysend, yrecv,
+    ffull, cfull, afull, twr, chalo, prod, pre, qrecv, ysend, yrecv,
     shifted, g, gsib, halfb, xin, full, fgsend, fgrecv,
     s_f, r_f, s_c, r_c, s_t, r_t, s_a, r_a, s_g, r_g,
-    s_h, r_h, s_q, r_q, s_y, r_y, s_core, r_core, s_x, r_x, s_ag, r_ag, s_fw, r_fw,
+    s_h, r_h, s_q, r_q, s_y, r_y, s_core, r_core, s_x, r_x, s_ag, r_ag, s_fw, r_fw, s_u, r_u,
 ):
     me = lax.axis_index("seq")
     z = lax.axis_index("tp")
@@ -93,25 +93,83 @@
             c.wait_recv()
 
     order = [1, nz - 1] + list(range(2, nz - 1))
-    cf = go([remote(fr, ffull.at[z], s_f.at[d], r_f.at[d], zpeer(d)) for d in order])
-    cc = go([remote(cot, cfull.at[z], s_c.at[d], r_c.at[d], zpeer(d)) for d in order])
-    ct = go([
-        remote(twt.at[lax.rem(z + d, nz)], twr.at[z], s_t.at[d], r_t.at[d], zpeer(d))
-        for d in order
-    ])
+    lh = loc // 2
+    hops = nz - 1
+
+    def line_copy(buf, ssem, rsem, way, h):
+        shard = z - h if way == 0 else z + h
+        return remote(
+            buf.at[shard], buf.at[shard], ssem.at[way, h], rsem.at[way, h],
+            {"tp": z + 1 if way == 0 else z - 1},
+        )
+
+    def can_send(way, h):
+        if way == 0:
+            return (z - h >= 0) & (z + 1 < nz)
+        return (z + h < nz) & (z - 1 >= 0)
+
+    def line_send(line, h):
+        for way in range(2):
+            @pl.when(can_send(way, h))
+            def _():
+                line_copy(*line, way, h).start()
+
+    def line_recv(line, h):
+        buf, ssem, rsem = line
+        for way in range(2):
+            shard = z - 1 - h if way == 0 else z + 1 + h
+
+            @pl.when(shard >= 0 if way == 0 else shard < nz)
+            def _():
+                remote(
+                    buf.at[shard], buf.at[shard], ssem.at[way, h], rsem.at[way, h],
+                    {"tp": z - 1 if way == 0 else z + 1},
+                ).wait_recv()
+
+    def line_step(line, h):
+        line_recv(line, h)
+        if h + 1 < hops:
+            line_send(line, h + 1)
+
+    def line_end(line):
+        for h in range(hops):
+            for way in range(2):
+                @pl.when(can_send(way, h))
+                def _():
+                    line_copy(*line, way, h).wait_send()
+
+    lf, lc, la = (ffull, s_f, r_f), (cfull, s_c, r_c), (afull, s_a, r_a)
+    ffull[z] = fr[...]
+    line_send(lf, 0)
+    cfull[z] = cot[...]
     ch = go([
         remote(cot, chalo.at[0], s_h.at[0], r_h.at[0], speer(1)),
         remote(cot, chalo.at[1], s_h.at[1], r_h.at[1], speer(-1)),
     ])
-    ffull[z] = fr[...]
-    cfull[z] = cot[...]
+    rows = pl.ds(pl.multiple_of(core * lh, 16), lh)
+    ct = go([
+        remote(
+            twt.at[lax.rem(z + d, nz), :, rows], twr.at[z, :, rows],
+            s_t.at[d], r_t.at[d], zpeer(d),
+        )
+        for d in order
+    ])
     twr[z] = twt[z]
     if 2 * hr > 3 * loc:
         for k in range(4):
             g[k, pl.ds(3 * loc, 2 * hr - 3 * loc), :] = jnp.zeros(
                 (2 * hr - 3 * loc, chans), F32
             )
-    arrived(cf)
+    line_step(lf, 0)
+    line_send(lc, 0)
+    for h in range(1, hops):
+        line_step(lf, h)
+        line_step(lc, h - 1)
+    cu = []
+    for k, d in enumerate(order):
+        ct[k].wait_recv()
+        part = twr.at[lax.rem(z + nz - d, nz), :, rows]
+        cu += go([remote(part, part, s_u.at[d], r_u.at[d], sib)])
 
     @pl.loop(0, 9)
     def _(t):
@@ -123,10 +181,9 @@
             total = total + moved(prod[t], t // 3 - 1, t % 3 - 1)
     pre[...] = total
     afull[z] = (total / (1.0 + jnp.exp(-total))).astype(BF)
-    ca = go([remote(afull.at[z], afull.at[z], s_a.at[d], r_a.at[d], zpeer(d)) for d in order])
-
-    arrived(cc)
-    arrived(ct)
+    line_send(la, 0)
+    line_step(lc, hops - 1)
+    arrived(cu)
 
     def back_of(k):
         acc = nn(twr[0, k], cfull[0])
@@ -134,15 +191,16 @@
             acc = acc + nn(twr[i, k], cfull[i])
         return acc
 
-    qsend[0] = back_of(0)
-    qsend[1] = back_of(2)
+    prod[5] = back_of(0)
+    prod[6] = back_of(2)
     cq = go([
-        remote(qsend.at[0], qrecv.at[0], s_q.at[0], r_q.at[0], speer(-1)),
-        remote(qsend.at[1], qrecv.at[1], s_q.at[1], r_q.at[1], speer(1)),
+        remote(prod.at[5], qrecv.at[0], s_q.at[0], r_q.at[0], speer(-1)),
+        remote(prod.at[6], qrecv.at[1], s_q.at[1], r_q.at[1], speer(1)),
     ])
-    qself[...] = back_of(1)
+    prod[8] = back_of(1)
+    line_step(la, 0)
     arrived(cq)
-    back = qself[...]
+    back = prod[8]
     back = back + jnp.where(me < ns - 1, qrecv[0], 0.0)
     back = back + jnp.where(me > 0, qrecv[1], 0.0)
     pr = pre[...]
@@ -150,6 +208,21 @@
     pg = (back * sg * (1.0 + pr * (1.0 - sg))).astype(BF).astype(F32)
     for t in range(9):
         shifted[t] = moved(pg, 1 - t // 3, 1 - t % 3).astype(BF)
+
+    if hops > 1:
+        line_step(la, 1)
+    prod[0:nz] = tn(cw[0], shifted[0]).reshape(nz, loc, -1)
+
+    @pl.loop(1, 9)
+    def _(t):
+        prod[0:nz] += tn(cw[t], shifted[t]).reshape(nz, loc, -1)
+
+    for i in range(nz):
+        fgsend[i] = prod[i].astype(BF)
+    cg = go([
+        remote(fgsend.at[lax.rem(z + d, nz)], fgrecv.at[d - 1], s_g.at[d], r_g.at[d], zpeer(d))
+        for d in order
+    ])
 
     other = pl.ds(pl.multiple_of((1 - core) * hr, 16), hr)
     mine = pl.ds(pl.multiple_of(core * hr, 16), hr)
@@ -201,7 +274,8 @@
             arrived(ccore[u - 1])
             cx[u - 1] = chip_send(u - 1)
 
-    arrived(ca)
+    for h in range(2, hops):
+        line_step(la, h)
     arrived(ch)
 
     def time_part(k, rows):
@@ -223,18 +297,6 @@
     arrived(ccore[3])
     cx[3] = chip_send(3)
 
-    prod[0:nz] = tn(cw[0], shifted[0]).reshape(nz, loc, -1)
-
-    @pl.loop(1, 9)
-    def _(t):
-        prod[0:nz] += tn(cw[t], shifted[t]).reshape(nz, loc, -1)
-
-    for i in range(nz):
-        fgsend[i] = prod[i].astype(BF)
-    cg = go([
-        remote(fgsend.at[lax.rem(z + d, nz)], fgrecv.at[d - 1], s_g.at[d], r_g.at[d], zpeer(d))
-        for d in order
-    ])
     for k in range(4):
         arrived(cx[k])
         cag[k] = chip_sum(k)
@@ -265,6 +327,8 @@
                 tgrad[v] = piece
     for c in everything:
         c.wait_send()
+    for line in (lf, lc, la):
+        line_end(line)
 
 
 def per_device(frames, conv_weight, time_weight, cotangent):
@@ -277,8 +341,8 @@
     twt = jnp.transpose(time_weight.reshape(3, loc, nz, loc), (2, 0, 3, 1))
     dma = pltpu.SemaphoreType.DMA
     V = pltpu.VMEM
-    sems = [dma((nz,))] * 10 + [dma((2,))] * 6 + [dma((4,))] * 2
-    sems += [dma((4, nc - 1))] * 4 + [dma((4,))] * 2
+    sems = [dma((2, nz))] * 4 + [dma((nz,))] * 2 + [dma((2, nz))] * 2 + [dma((nz,))] * 2 + [dma((2,))] * 6 + [dma((4,))] * 2
+    sems += [dma((4, nc - 1))] * 4 + [dma((4,))] * 2 + [dma((nz,))] * 2
     outs = pl.pallas_call(
         functools.partial(kernel, ns, nz, q),
         out_shape=(
@@ -297,8 +361,6 @@
             V((2, loc, plane), BF),
             V((9, loc, plane), F32),
             V((loc, plane), F32),
-            V((loc, plane), F32),
-            V((2, loc, plane), F32),
             V((2, loc, plane), F32),
             V((2, loc, plane), BF),
             V((2, loc, plane), BF),

time: 178 us -> 141 us (0.79)
  Pallas kernels: 163 us -> 126 us
    pallas_call x1, Pallas kernels: 163 us -> 126 us  [per_device(): pl.pallas_call(functools.partial(kernel, ns, nz, q), out_shape=(jax.Shape...]
where the time goes in v2:
time: 141 us
  Pallas kernels  126 us (89%)
  local copies, waits for them, and re-layouts  13.4 us (10%)
    pallas_call x1, Pallas kernels, per_device(): pl.pallas_call(functools.partial(kernel, ns, nz, q), out_shape=(jax.Shape...  126 us
    unnamed x6, local copies, waits for them, and re-layouts  8.69 us
    reshape x2, local copies, waits for them, and re-layouts, per_device(): twt = jnp.transpose(time_weight.reshape(3, loc, nz, loc), (2, 0, 3, 1))  4.71 us

profile of v2, /device:TPU:1, one launch (start us, length us, event | category | flops | bytes accessed | tf_op | source)
XLA Modules:
  0.0 140.5 jit_solution(17891030609406851128)
XLA Ops:
  0.6 2.7 %reshape.24 = bf16[3,160,4,160]{3,2,1,0:T(4,128)(2,1)S(1)} reshape(bf16[3,160,640]{2,1,0:T(8,128)(2,1)} %tw.1) | data formatting | bytes 1228800 | tf_op jit(solution)/shard_map/reshape | solution.py:341
  3.3 2.0 %copy.8 = bf16[3,160,4,160]{1,3,0,2:T(8,128)(2,1)} copy(bf16[3,160,4,160]{3,2,1,0:T(4,128)(2,1)S(1)} %reshape.24) | data formatting | bytes 1228800 | tf_op jit(solution)/shard_map/reshape | solution.py:341
  5.3 126.5 %shard_map.75 = (bf16[160,1024]{1,0:T(8,128)(2,1)}, bf16[160,1024]{1,0:T(8,128)(2,1)}, f32[9,160,640]{2,1,0:T(8,128)}, f32[3,160,640]{2,1,0:T(8,128)}) custom-call(bf16[160,1024]{1,0:T(8,128)(2,1)} %bitcast.8, bf16[9,160,640]{2,1,0:T(8,128)(2,1)} %cw.1, bf16[3,160,640]{2,1,0:T(8,128)(2,1)} %tw.1, bf16[4,3,160,160]{3,2,1,0:T(8,128)(2,1)} %bitcast.5, ...), custom_call_target="tpu_custom_call" | custom-call | tf_op jit(solution)/shard_map/pallas_call | solution.py:346
  131.8 1.7 %copy.13 = bf16[160,1,1024]{2,0,1:T(8,128)(2,1)} copy(bf16[160,1,1024]{2,0,1:T(8,128)(2,1)} %bitcast.7) | data formatting | bytes 655360
  133.5 1.7 %copy.14 = bf16[160,1,1024]{2,0,1:T(8,128)(2,1)} copy(bf16[160,1,1024]{2,0,1:T(8,128)(2,1)} %bitcast.6) | data formatting | bytes 655360
  135.3 0.0 copy-start
  135.3 4.2 %copy.15 = f32[9,160,640]{2,1,0:T(8,128)} copy(f32[9,160,640]{2,1,0:T(8,128)} %get-tuple-element.18) | data formatting | bytes 7372800
  139.5 0.0 copy-done
  139.5 1.0 copy.16
Async XLA Ops:
  135.3 4.2 %copy-start = (f32[3,160,640]{2,1,0:T(8,128)S(1)}, f32[3,160,640]{2,1,0:T(8,128)}, u32[]{:S(2)}) copy-start(f32[3,160,640]{2,1,0:T(8,128)} %get-tuple-element.19) | copy-start | bytes 3686404

commit v3 on v2

--- a/solution.py
+++ b/solution.py
@@ -40,9 +40,9 @@
 
 def kernel(
     ns, nz, q,
-    fr, cw, tw, twt, cot,
+    fr, cw, tw, cot,
     out, fgrad, cgrad, tgrad,
-    ffull, cfull, afull, twr, chalo, prod, pre, qrecv, ysend, yrecv,
+    ffull, cfull, afull, twt, twr, chalo, prod, pre, qrecv, ysend, yrecv,
     shifted, g, gsib, halfb, xin, full, fgsend, fgrecv,
     s_f, r_f, s_c, r_c, s_t, r_t, s_a, r_a, s_g, r_g,
     s_h, r_h, s_q, r_q, s_y, r_y, s_core, r_core, s_x, r_x, s_ag, r_ag, s_fw, r_fw, s_u, r_u,
@@ -147,6 +147,9 @@
         remote(cot, chalo.at[1], s_h.at[1], r_h.at[1], speer(-1)),
     ])
     rows = pl.ds(pl.multiple_of(core * lh, 16), lh)
+    for i in range(nz):
+        for k in range(3):
+            twt[i, k] = tw[k, :, i * loc:(i + 1) * loc]
     ct = go([
         remote(
             twt.at[lax.rem(z + d, nz), :, rows], twr.at[z, :, rows],
@@ -186,9 +189,9 @@
     arrived(cu)
 
     def back_of(k):
-        acc = nn(twr[0, k], cfull[0])
+        acc = tn(twr[0, k], cfull[0])
         for i in range(1, nz):
-            acc = acc + nn(twr[i, k], cfull[i])
+            acc = acc + tn(twr[i, k], cfull[i])
         return acc
 
     prod[5] = back_of(0)
@@ -320,7 +323,7 @@
     for k in range(4):
         arrived(cfw[k])
         for v in range(3):
-            piece = full[k, v * loc:(v + 1) * loc, :].astype(F32) / ns
+            piece = full[k, v * loc:(v + 1) * loc, :]
             if k < 3:
                 cgrad[3 * k + v] = piece
             else:
@@ -332,13 +335,12 @@
 
 
 def per_device(frames, conv_weight, time_weight, cotangent):
-    loc, count, plane = frames.shape
+    loc, _, plane = frames.shape
     ns, nz = lax.axis_size("seq"), lax.axis_size("tp")
     chans = conv_weight.shape[2]
     q = 16 * (-(-3 * loc // (16 * ns)))
     nc = ns // 2
     hr = nc * q
-    twt = jnp.transpose(time_weight.reshape(3, loc, nz, loc), (2, 0, 3, 1))
     dma = pltpu.SemaphoreType.DMA
     V = pltpu.VMEM
     sems = [dma((2, nz))] * 4 + [dma((nz,))] * 2 + [dma((2, nz))] * 2 + [dma((nz,))] * 2 + [dma((2,))] * 6 + [dma((4,))] * 2
@@ -348,15 +350,16 @@
         out_shape=(
             jax.ShapeDtypeStruct((loc, plane), BF),
             jax.ShapeDtypeStruct((loc, plane), BF),
-            jax.ShapeDtypeStruct((9, loc, chans), F32),
-            jax.ShapeDtypeStruct((3, loc, chans), F32),
+            jax.ShapeDtypeStruct((9, loc, chans), BF),
+            jax.ShapeDtypeStruct((3, loc, chans), BF),
         ),
-        in_specs=[pl.BlockSpec(memory_space=pltpu.VMEM)] * 5,
+        in_specs=[pl.BlockSpec(memory_space=pltpu.VMEM)] * 4,
         out_specs=(pl.BlockSpec(memory_space=pltpu.VMEM),) * 4,
         scratch_shapes=[
             V((nz, loc, plane), BF),
             V((nz, loc, plane), BF),
             V((nz, loc, plane), BF),
+            V((nz, 3, loc, loc), BF),
             V((nz, 3, loc, loc), BF),
             V((2, loc, plane), BF),
             V((9, loc, plane), F32),
@@ -377,11 +380,12 @@
             collective_id=0, has_side_effects=True, vmem_limit_bytes=58 * 1024 * 1024
         ),
     )(
-        frames.reshape(loc, plane), conv_weight, time_weight, twt,
+        frames.reshape(loc, plane), conv_weight, time_weight,
         cotangent.reshape(loc, plane),
     )
     return (
-        outs[0].reshape(frames.shape), outs[1].reshape(frames.shape), outs[2], outs[3],
+        outs[0].reshape(frames.shape), outs[1].reshape(frames.shape),
+        outs[2].astype(F32) / ns, outs[3].astype(F32) / ns,
     )
 
 

time: 141 us -> 133 us (0.943)
  local copies, waits for them, and re-layouts: 13.4 us -> 1.46 us
  other arithmetic: 0 us -> 4.81 us
    unnamed x6 -> x8, local copies, waits for them, and re-layouts: 8.69 us -> 1.46 us
    div x0 -> x2, other arithmetic: none -> 4.81 us  [the longest x1 3.7 us: per_device(): outs[2].astype(F32) / ns]
    reshape x2 -> x0, local copies, waits for them, and re-layouts: 4.71 us -> none  [per_device(): twt = jnp.transpose(time_weight.reshape(3, loc, nz, loc), (2, 0, 3, 1))]
where the time goes in v3:
time: 133 us; the launch traced here: 132 us
  Pallas kernels  125 us (94%)
  other arithmetic  4.81 us (4%)
  local copies, waits for them, and re-layouts  1.46 us (1%)
    pallas_call x1, Pallas kernels, per_device(): pl.pallas_call(functools.partial(kernel, ns, nz, q), out_shape=(jax.Shape...  125 us
    div x1, other arithmetic, per_device(): outs[2].astype(F32) / ns  3.7 us

profile of v3, /device:TPU:1, one launch (start us, length us, event | category | flops | bytes accessed | tf_op | source)
XLA Modules:
  0.0 132.4 jit_solution(14576846895376408157)
XLA Ops:
  0.6 125.5 %shard_map.75 = (bf16[160,1024]{1,0:T(8,128)(2,1)}, bf16[160,1024]{1,0:T(8,128)(2,1)}, bf16[9,160,640]{2,1,0:T(8,128)(2,1)}, bf16[3,160,640]{2,1,0:T(8,128)(2,1)}) custom-call(bf16[160,1024]{1,0:T(8,128)(2,1)} %bitcast.4, bf16[9,160,640]{2,1,0:T(8,128)(2,1)} %cw.1, bf16[3,160,640]{2,1,0:T(8,128)(2,1)} %tw.1, bf16[160,1024]{1,0:T(8,128)(2,1)} %bitcast.5), custom_call_target="tpu_custom_call" | custom-call | tf_op jit(solution)/shard_map/pallas_call | solution.py:348
  126.1 0.0 copy-start
  126.1 3.7 %convert_multiply_fusion = f32[9,160,640]{2,1,0:T(8,128)} fusion(bf16[9,160,640]{2,1,0:T(8,128)(2,1)} %get-tuple-element.10), kind=kLoop, calls=%fused_computation | loop fusion | flops 1843200 | bytes 5529600 | tf_op jit(solution)/shard_map/div | solution.py:388
  129.8 0.0 copy-start.2
  129.8 0.0 copy-start.1
  129.8 0.0 copy-done
  129.8 1.1 convert_multiply_fusion.1
  130.9 0.0 copy-done.2
  130.9 0.7 copy.10
  131.7 0.0 copy-done.1
  131.7 0.7 copy.11
Async XLA Ops:
  126.1 3.7 %copy-start = (bf16[3,160,640]{2,1,0:T(8,128)(2,1)S(1)}, bf16[3,160,640]{2,1,0:T(8,128)(2,1)}, u32[]{:S(2)}) copy-start(bf16[3,160,640]{2,1,0:T(8,128)(2,1)} %get-tuple-element.11) | copy-start | bytes 1843204
  129.8 1.1 copy-start.2
  129.8 1.8 %copy-start.1 = (bf16[160,1024]{1,0:T(8,128)(2,1)S(1)}, bf16[160,1024]{1,0:T(8,128)(2,1)}, u32[]{:S(2)}) copy-start(bf16[160,1024]{1,0:T(8,128)(2,1)} %get-tuple-element.9) | copy-start | bytes 983044

commit v4 on v3

--- a/solution.py
+++ b/solution.py
@@ -212,14 +212,14 @@
     for t in range(9):
         shifted[t] = moved(pg, 1 - t // 3, 1 - t % 3).astype(BF)
 
-    if hops > 1:
-        line_step(la, 1)
     prod[0:nz] = tn(cw[0], shifted[0]).reshape(nz, loc, -1)
 
     @pl.loop(1, 9)
     def _(t):
         prod[0:nz] += tn(cw[t], shifted[t]).reshape(nz, loc, -1)
 
+    if hops > 1:
+        line_step(la, 1)
     for i in range(nz):
         fgsend[i] = prod[i].astype(BF)
     cg = go([
@@ -277,6 +277,11 @@
             arrived(ccore[u - 1])
             cx[u - 1] = chip_send(u - 1)
 
+    arrived(ccore[2])
+    cx[2] = chip_send(2)
+    for k in range(2):
+        arrived(cx[k])
+        cag[k] = chip_sum(k)
     for h in range(2, hops):
         line_step(la, h)
     arrived(ch)
@@ -288,8 +293,6 @@
     time_part(1, cot[...])
     time_part(2, jnp.where(me > 0, chalo[0], jnp.zeros_like(chalo[0])))
     ccore[3] = core_send(3)
-    arrived(ccore[2])
-    cx[2] = chip_send(2)
 
     ysend[0] = nn(tw[0], afull[...].reshape(chans, -1)).astype(BF)
     ysend[1] = nn(tw[2], afull[...].reshape(chans, -1)).astype(BF)
@@ -300,7 +303,7 @@
     arrived(ccore[3])
     cx[3] = chip_send(3)
 
-    for k in range(4):
+    for k in range(2, 4):
         arrived(cx[k])
         cag[k] = chip_sum(k)
 

time: 133 us -> 132 us (level)
  no operation moved by 1% of the time
where the time goes in v4:
time: 132 us
  Pallas kernels  125 us (95%)
  other arithmetic  4.81 us (4%)
  local copies, waits for them, and re-layouts  1.46 us (1%)
    pallas_call x1, Pallas kernels, per_device(): pl.pallas_call(functools.partial(kernel, ns, nz, q), out_shape=(jax.Shape...  125 us
    div x1, other arithmetic, per_device(): outs[2].astype(F32) / ns  3.7 us

profile of v4, /device:TPU:1, one launch (start us, length us, event | category | flops | bytes accessed | tf_op | source)
XLA Modules:
  0.0 131.9 jit_solution(6827023746618679008)
XLA Ops:
  0.6 125.0 %shard_map.75 = (bf16[160,1024]{1,0:T(8,128)(2,1)}, bf16[160,1024]{1,0:T(8,128)(2,1)}, bf16[9,160,640]{2,1,0:T(8,128)(2,1)}, bf16[3,160,640]{2,1,0:T(8,128)(2,1)}) custom-call(bf16[160,1024]{1,0:T(8,128)(2,1)} %bitcast.4, bf16[9,160,640]{2,1,0:T(8,128)(2,1)} %cw.1, bf16[3,160,640]{2,1,0:T(8,128)(2,1)} %tw.1, bf16[160,1024]{1,0:T(8,128)(2,1)} %bitcast.5), custom_call_target="tpu_custom_call" | custom-call | tf_op jit(solution)/shard_map/pallas_call | solution.py:351
  125.6 0.0 copy-start
  125.7 3.7 %convert_multiply_fusion = f32[9,160,640]{2,1,0:T(8,128)} fusion(bf16[9,160,640]{2,1,0:T(8,128)(2,1)} %get-tuple-element.10), kind=kLoop, calls=%fused_computation | loop fusion | flops 1843200 | bytes 5529600 | tf_op jit(solution)/shard_map/div | solution.py:391
  129.4 0.0 copy-start.2
  129.4 0.0 copy-start.1
  129.4 0.0 copy-done
  129.4 1.1 convert_multiply_fusion.1
  130.5 0.0 copy-done.2
  130.5 0.7 copy.10
  131.2 0.0 copy-done.1
  131.2 0.7 copy.11
Async XLA Ops:
  125.6 3.7 %copy-start = (bf16[3,160,640]{2,1,0:T(8,128)(2,1)S(1)}, bf16[3,160,640]{2,1,0:T(8,128)(2,1)}, u32[]{:S(2)}) copy-start(bf16[3,160,640]{2,1,0:T(8,128)(2,1)} %get-tuple-element.11) | copy-start | bytes 1843204
  129.4 1.1 copy-start.2
  129.4 1.8 %copy-start.1 = (bf16[160,1024]{1,0:T(8,128)(2,1)S(1)}, bf16[160,1024]{1,0:T(8,128)(2,1)}, u32[]{:S(2)}) copy-start(bf16[160,1024]{1,0:T(8,128)(2,1)} %get-tuple-element.9) | copy-start | bytes 983044
